TPU v7x, 32 devices: a whole 2x2x4 slice. The times are simulated.
32 devices in a mesh: grp: 2 (over y), row: 8 (over z, x), col: 2 (over core).
Axes of the slice: x: 2, y: 2, z: 4, core: 2. Of those that a mesh axis runs over, the one named last changes fastest.
Arguments:
- queries: bfloat16 [1024, 8192], P(('grp', 'row'), 'col'), parts along dimension 0, may hold values from -256 to 256
- key_cache: bfloat16 [512, 512], P(('grp', 'row', 'col')), parts along dimension 0, may hold values from -6 to 6
- value_cache: bfloat16 [512, 512], P(('grp', 'row', 'col')), parts along dimension 0, may hold values from -6 to 6
- tile_active: int32 [8, 2], P('grp'), parts along dimension 0, may hold values from 0 to 1, as said below
- query_step: int32 [1024], P(('grp', 'row')), parts along dimension 0, may hold values from 0 to 63
- key_step: int32 [512], P(('grp', 'row', 'col')), parts along dimension 0, may hold values from 0 to 63, never falling along the last dimension, each value on 1 to 16 neighbouring positions
Outputs:
- attended: bfloat16 [1024, 8192], P(('grp', 'row'), 'col'), parts along dimension 0
There are 2 independent parts, one for each index of `grp`. A program takes and returns all parts, laid end to end along the dimension named above; each array names one. Nothing has to cross between parts.
Inputs may be any that keep to these rules, and one draw needn't show every extreme that they name: `tile_active`: every entry of column 0 is 1. `key_step`: never falls along the cached rows and starts at 0.
All inputs are finite; a program needn't handle non-finite values.
Results may differ from a plain program's by a relative error of at most 0.015.
Values may be sent and summed in bfloat16 or wider, within the bound.
A program may use at most 64 MiB of HBM per device.

v0:
```python
import math

import jax
import jax.numpy as jnp
from jax import lax
from jax.sharding import PartitionSpec as P

H = 64
KVH = 4
DH = 128
TILE = 128


def arrange(matrix, head_count, groups):
    row_count = matrix.shape[0]
    shaped = matrix.reshape(row_count, head_count, groups, DH).transpose(1, 2, 0, 3)
    return shaped.reshape(head_count, groups * row_count, DH)


def initial(head_count, row_count):
    return (
        jnp.full((head_count, row_count), -1e30, jnp.float32),
        jnp.zeros((head_count, row_count), jnp.float32),
        jnp.zeros((head_count, row_count, DH), jnp.float32),
    )


def make_folder(grouped, tile_rows, query_step, place, scaling):
    head_count = grouped.shape[0]
    groups = grouped.shape[1] // query_step.shape[0]
    tile_total = tile_rows.shape[1]

    def update(running, block):
        keys_block, values_block, marks_block, positions = block
        highest, totals, numerator = running
        scores = (
            jnp.einsum("hqd,hkd->hqk", grouped, keys_block, preferred_element_type=jnp.float32)
            * scaling
        )
        onehot = (
            jnp.arange(tile_total, dtype=jnp.int32)[:, None] == (positions // TILE)[None, :]
        ).astype(jnp.float32)
        tile_ok = jnp.dot(tile_rows, onehot, preferred_element_type=jnp.float32) > 0.5
        step_ok = marks_block.astype(jnp.int32)[None, :] <= query_step[:, None]
        allowed = jnp.tile(tile_ok & step_ok, (groups, 1))[None]
        scores = jnp.where(allowed, scores, -1e30)
        newest = jnp.maximum(highest, jnp.max(scores, axis=-1))
        weights = jnp.where(allowed, jnp.exp(scores - newest[..., None]), 0.0)
        factor = jnp.exp(highest - newest)
        totals = totals * factor + jnp.sum(weights, axis=-1)
        numerator = numerator * factor[..., None] + jnp.einsum(
            "hqk,hkd->hqd",
            weights.astype(jnp.bfloat16),
            values_block,
            preferred_element_type=jnp.float32,
        )
        return ((newest, totals, numerator), None)

    def folder(running, piece, start):
        keys_piece, values_piece, marks_piece = piece
        count = keys_piece.shape[0]
        width = 512 if count % 512 == 0 else count
        blocks = count // width
        positions = place(jnp.arange(count, dtype=jnp.int32))

        def split_heads(array):
            return array.reshape(blocks, width, head_count, DH).transpose(0, 2, 1, 3)

        stacked = (
            split_heads(keys_piece),
            split_heads(values_piece),
            marks_piece.reshape(blocks, width),
            positions.reshape(blocks, width),
        )
        running, ignored = lax.scan(update, running, stacked)
        return running

    return folder


def same_place(index):
    return index


def per_device(queries, key_cache, value_cache, tile_active, query_step, key_step):
    groups = H // KVH
    scaling = 1.0 / math.sqrt(DH)
    query_count = queries.shape[0]
    key_local = key_cache.shape[0]
    columns = lax.axis_size("col")
    local_heads = KVH // columns
    first_row = lax.axis_index("row") * query_count
    query_tiles = (first_row + jnp.arange(query_count, dtype=jnp.int32)) // TILE
    tile_total = tile_active.shape[0]
    picker = (query_tiles[:, None] == jnp.arange(tile_total, dtype=jnp.int32)[None, :]).astype(
        jnp.float32
    )
    tile_rows = jnp.dot(picker, tile_active.astype(jnp.float32), preferred_element_type=jnp.float32)
    step_marks = key_step.astype(jnp.bfloat16)
    wide_marks = jnp.broadcast_to(step_marks[:, None], (key_local, columns))
    key_part, value_part, mark_part = (
        lax.all_to_all(key_cache, "col", split_axis=1, concat_axis=0, tiled=True),
        lax.all_to_all(value_cache, "col", split_axis=1, concat_axis=0, tiled=True),
        lax.all_to_all(wide_marks, "col", split_axis=1, concat_axis=0, tiled=True),
    )
    grouped = arrange(queries, local_heads, groups)
    folder = make_folder(grouped, tile_rows, query_step, same_place, scaling)
    running = folder(
        initial(local_heads, groups * query_count),
        (
            lax.all_gather(key_part, "row", axis=0, tiled=True),
            lax.all_gather(value_part, "row", axis=0, tiled=True),
            lax.all_gather(mark_part.reshape(-1), "row", axis=0, tiled=True),
        ),
        jnp.int32(0),
    )
    numerator = running[2]
    totals = running[1]
    result = numerator / totals[..., None]
    result = result.reshape(local_heads, groups, query_count, DH).transpose(2, 0, 1, 3)
    return result.reshape(query_count, local_heads * groups * DH).astype(jnp.bfloat16)


def solution(mesh):
    in_specs = (
        P(("grp", "row"), "col"),
        P(("grp", "row", "col"), None),
        P(("grp", "row", "col"), None),
        P("grp", None),
        P(("grp", "row")),
        P(("grp", "row", "col")),
    )
    out_specs = P(("grp", "row"), "col")
    return jax.shard_map(
        per_device, mesh=mesh, in_specs=in_specs, out_specs=out_specs, check_vma=False
    )
```

profile of v0, /device:TPU:0, one launch (start us, length us, event | category | flops | bytes accessed | tf_op | source)
XLA Modules:
  0.0 106.9 jit_solution(8074432039066238169)
XLA Ops:
  0.0 0.7 convert_element_type.32
  0.7 0.6 broadcast_in_dim.53
  1.3 3.2 %all-to-all-start = ((bf16[16,2,1]{0,2,1:T(2,128)(2,1)}), bf16[16,2,1]{0,2,1:T(2,128)(2,1)S(1)}, u32[]{:S(2)}, u32[]{:S(2)}) async-start(bf16[16,2,1]{0,2,1:T(2,128)(2,1)} %broadcast_in_dim.53), calls=%async_computation | async-start | bytes 2048 | tf_op jit(solution)/shard_map/all_to_all | solution.py:104
  4.5 1.3 %copy.59 = bf16[2,2,8,256]{3,2,0,1:T(8,128)(2,1)} copy(bf16[2,2,8,256]{3,2,1,0:T(8,128)(2,1)} %bitcast.57) | data formatting | bytes 32768 | tf_op jit(solution)/shard_map/all_to_all | solution.py:102
  5.8 3.2 %all-to-all-start.1 = ((bf16[16,2,256]{2,0,1:T(8,128)(2,1)}), bf16[16,2,256]{2,0,1:T(8,128)(2,1)S(1)}, u32[]{:S(2)}, u32[]{:S(2)}) async-start(bf16[16,2,256]{2,0,1:T(8,128)(2,1)} %bitcast.46), calls=%async_computation.1 | async-start | bytes 32768 | tf_op jit(solution)/shard_map/all_to_all | solution.py:102
  9.2 1.3 %dynamic-slice.3 = u32[1]{0:T(128)} dynamic-slice(u32[32]{0:T(128)} %constant.72, u32[]{:T(128)S(6)} %add.38), dynamic_slice_sizes={1} | dynamic-slice | bytes 12
  11.2 0.2 dynamic-update-slice
  11.5 23.1 %all-reduce = bf16[256]{0:T(256)(128)(2,1)S(1)} all-reduce(bf16[256]{0:T(256)(128)(2,1)S(1)} %dynamic-update-slice), channel_id=1, replica_groups=mesh['grp'=2,'row'=8,'col'=2] {'row'}, use_global_device_ids=true, to_apply=%add | all-reduce | flops 256 | bytes 1024
  34.6 1.1 %fusion.5 = pred[64,256]{1,0:T(8,128)(4,1)S(1)} fusion(s32[256]{0:T(256)S(1)} %convert_element_type.33, s32[64]{0:T(128)} %param.10, s32[64]{0:T(128)S(1)} %and_select_fusion.1, s32[256]{0:T(256)S(1)} %and_select_fusion, s32[4,2]{0,1:T(2,128)} %param.9), kind=kOutput, calls=%fused_computation.9 | convolution fusion | flops 116488 | bytes 18976 | tf_op jit(solution)/shard_map/while/body/eval_jaxpr/dot_general | solution.py:43
  35.8 0.4 copy.39
  36.2 1.1 %copy.52 = bf16[8,8,32,128]{3,2,1,0:T(8,128)(2,1)S(1)} copy(bf16[8,8,32,128]{3,1,2,0:T(8,128)(2,1)} %bitcast.51) | data formatting | bytes 1048576
  37.3 0.2 copy.40
  37.6 0.6 copy.58
  38.2 3.2 %all-to-all-start.2 = ((bf16[16,2,256]{2,0,1:T(8,128)(2,1)}), bf16[16,2,256]{2,0,1:T(8,128)(2,1)S(1)}, u32[]{:S(2)}, u32[]{:S(2)}) async-start(bf16[16,2,256]{2,0,1:T(8,128)(2,1)} %bitcast.45), calls=%async_computation.2 | async-start | bytes 32768 | tf_op jit(solution)/shard_map/all_to_all | solution.py:103
  41.4 30.5 %all_gather.10 = bf16[256,256]{1,0:T(8,128)(2,1)S(1)} all-gather(bf16[32,256]{1,0:T(8,128)(2,1)S(1)} %bitcast.55), channel_id=1, replica_groups=mesh['grp'=2,'row'=8,'col'=2] {'row'}, dimensions={0}, use_global_device_ids=true | all-gather | bytes 147456 | tf_op jit(solution)/shard_map/all_gather | solution.py:111
  71.9 0.1 copy.42
  72.0 0.1 copy.43
  72.1 0.6 fusion
  72.7 0.6 fusion.1
  73.3 30.5 %all_gather.11 = bf16[256,256]{1,0:T(8,128)(2,1)S(1)} all-gather(bf16[32,256]{1,0:T(8,128)(2,1)S(1)} %bitcast.56), channel_id=1, replica_groups=mesh['grp'=2,'row'=8,'col'=2] {'row'}, dimensions={0}, use_global_device_ids=true | all-gather | bytes 147456 | tf_op jit(solution)/shard_map/all_gather | solution.py:112
  104.0 0.1 copy.46
  104.1 1.4 %fusion.4 = bf16[2,1024,128]{2,1,0:T(8,128)(2,1)S(1)} fusion(f32[2,1024,256]{1,2,0:T(8,128)S(1)} %get-tuple-element.28, f32[2,1024]{1,0:T(2,128)S(1)} %broadcast_maximum_fusion, pred[1024,256]{0,1:T(8,128)(4,1)S(1)} %copy.39, f32[2,1024]{1,0:T(2,128)S(1)} %get-tuple-element.26, f32[2,1024]{1,0:T(2,128)S(1)} %get-tuple-element.25, ...), kind=kOutput, calls=%fused_computation.7 | convolution fusion | flops 137625600 | bytes 3039232 | tf_op jit(solution)/shard_map/while/body/eval_jaxpr/hqk,hkd->hqd/dot_general | solution.py:51
  105.5 0.3 copy.48
  105.9 1.0 copy.57
  (15 shorter events, 0.4 us)
Async XLA Ops:
  0.0 37.5 %copy-start = (bf16[16,512]{1,0:T(8,128)(2,1)S(1)}, bf16[16,512]{1,0:T(8,128)(2,1)}, u32[]{:S(2)}) copy-start(bf16[16,512]{1,0:T(8,128)(2,1)} %param.8) | copy-start | bytes 49156
  1.3 4.6 %all-to-all-start = ((bf16[16,2,1]{0,2,1:T(2,128)(2,1)}), bf16[16,2,1]{0,2,1:T(2,128)(2,1)S(1)}, u32[]{:S(2)}, u32[]{:S(2)}) async-start(bf16[16,2,1]{0,2,1:T(2,128)(2,1)} %broadcast_in_dim.53), calls=%async_computation | async-start | bytes 2048 | tf_op jit(solution)/shard_map/all_to_all | solution.py:104
  5.8 32.3 %all-to-all-start.1 = ((bf16[16,2,256]{2,0,1:T(8,128)(2,1)}), bf16[16,2,256]{2,0,1:T(8,128)(2,1)S(1)}, u32[]{:S(2)}, u32[]{:S(2)}) async-start(bf16[16,2,256]{2,0,1:T(8,128)(2,1)} %bitcast.46), calls=%async_computation.1 | async-start | bytes 32768 | tf_op jit(solution)/shard_map/all_to_all | solution.py:102
  38.2 35.2 %all-to-all-start.2 = ((bf16[16,2,256]{2,0,1:T(8,128)(2,1)}), bf16[16,2,256]{2,0,1:T(8,128)(2,1)S(1)}, u32[]{:S(2)}, u32[]{:S(2)}) async-start(bf16[16,2,256]{2,0,1:T(8,128)(2,1)} %bitcast.45), calls=%async_computation.2 | async-start | bytes 32768 | tf_op jit(solution)/shard_map/all_to_all | solution.py:103
where the time goes:
time: 107 us
  blocking collectives  84.1 us (79%)
  starting transfers between devices  9.69 us (9%)
  local copies, waits for them, and re-layouts  7.83 us (7%)
  matrix products  3.06 us (3%)
  other arithmetic  1.29 us (1%)
    all_gather x1, blocking collectives, per_device(): lax.all_gather(key_part, 'row', axis=0, tiled=True)  30.5 us
    all_gather x1, blocking collectives, per_device(): lax.all_gather(value_part, 'row', axis=0, tiled=True)  30.5 us
    unnamed x1, blocking collectives  23.1 us
    unnamed x7, local copies, waits for them, and re-layouts  3.71 us
    all_to_all x1, starting transfers between devices, per_device(): lax.all_to_all(key_cache, 'col', split_axis=1, concat_axis=0, tiled=True)  3.24 us
    all_to_all x1, starting transfers between devices, per_device(): lax.all_to_all(value_cache, 'col', split_axis=1, concat_axis=0, tiled=True)  3.23 us
    all_to_all x1, starting transfers between devices, per_device(): lax.all_to_all(wide_marks, 'col', split_axis=1, concat_axis=0, tiled=True)  3.22 us
  transfers between devices with their start and end apart: 3, of which 0 were waited for; matrix products, arithmetic and copies ran while one was open for 7% of the time, Pallas kernels for 0%

commit v1 on v0

v1 whole, which is shorter than its diff:
```python
import functools
import math

import jax
import jax.numpy as jnp
from jax import lax
from jax.experimental import pallas as pl
from jax.experimental.pallas import tpu as pltpu
from jax.sharding import PartitionSpec as P

H = 64
KVH = 4
DH = 128
TILE = 128
STEPS = 64
LOW = -1e30
MESH = pl.DeviceIdType.MESH


def repeat(count, body):
    if count <= 32:
        for index in range(count):
            body(index)
    else:
        lax.fori_loop(0, count, lambda index, nothing: (body(index), nothing)[1], 0)


def attend(q, kv_ref, bias_ref, head, heads, peers, scale):
    depth = kv_ref.shape[1]
    rows = q.shape[0]
    copies = rows // bias_ref.shape[0]
    span = min(peers, max(1, 512 // depth))

    def piece(first):
        keys = kv_ref[pl.ds(first, span), :, head * DH : (head + 1) * DH]
        values = kv_ref[pl.ds(first, span), :, (heads + head) * DH : (heads + head + 1) * DH]
        keys = keys.reshape(span * depth, DH)
        values = values.reshape(span * depth, DH)
        values = jnp.concatenate([values, jnp.ones_like(values)], axis=1)
        scores = lax.dot_general(q, keys, (((1,), (1,)), ((), ())), preferred_element_type=jnp.float32)
        return scores * scale, values

    if span == peers:
        scores, values = piece(0)
        bias = bias_ref[...]
        scores = scores + jnp.concatenate([bias] * copies, axis=0)
        top = jnp.max(scores, axis=1, keepdims=True)
        weights = jnp.exp2(scores - top).astype(jnp.bfloat16)
        both = jnp.dot(weights, values, preferred_element_type=jnp.float32)
    else:
        width = span * depth

        def step(index, carry):
            top, both = carry
            scores, values = piece(index * span)
            bias = bias_ref[:, pl.ds(pl.multiple_of(index * width, width), width)]
            scores = scores + jnp.concatenate([bias] * copies, axis=0)
            newest = jnp.maximum(top, jnp.max(scores, axis=1, keepdims=True))
            weights = jnp.where(scores > 0.5 * LOW, jnp.exp2(scores - newest), 0.0).astype(jnp.bfloat16)
            both = both * jnp.exp2(top - newest) + jnp.dot(weights, values, preferred_element_type=jnp.float32)
            return newest, both

        top = jnp.full((rows, 1), LOW, jnp.float32)
        top, both = lax.fori_loop(0, peers // span, step, (top, jnp.zeros((rows, 2 * DH), jnp.float32)))
    return both[:, :DH] / both[:, DH:]


def kernel(
    row_count, columns, q_hbm, k_ref, v_ref, tile_ref, qstep_ref, kstep_ref, out_ref,
    q_ref, send_ref, kv_ref, bias_ref, q_sem, send_sem, recv_sem,
):
    peers = row_count * columns
    heads = KVH // columns
    half = heads * DH
    groups = H // KVH
    depth = k_ref.shape[0]
    keys = peers * depth
    query_count = q_ref.shape[0]
    row = lax.axis_index("row")
    col = lax.axis_index("col")
    me = row * columns + col

    q_copy = pltpu.make_async_copy(q_hbm, q_ref, q_sem)
    q_copy.start()

    def place(distance):
        peer = lax.rem(me + distance + 1, peers)
        return peer, peer // columns, lax.rem(peer, columns)

    barrier = pltpu.get_barrier_semaphore()

    def greet(distance):
        peer, peer_row, peer_col = place(distance)
        pl.semaphore_signal(barrier, inc=1, device_id={"row": peer_row, "col": peer_col}, device_id_type=MESH)

    repeat(peers - 1, greet)

    steps = kstep_ref[...].astype(jnp.float32)
    eye = lax.broadcasted_iota(jnp.int32, (depth, depth), 0) == lax.broadcasted_iota(jnp.int32, (depth, depth), 1)
    column = jnp.sum(jnp.where(eye, jnp.broadcast_to(steps, (depth, depth)), 0.0), axis=1, keepdims=True)
    marks = jnp.broadcast_to(column, (depth, DH)).astype(jnp.bfloat16)
    for other in range(columns):
        send_ref[other, :, :half] = k_ref[:, other * half : (other + 1) * half]
        send_ref[other, :, half : 2 * half] = v_ref[:, other * half : (other + 1) * half]
        send_ref[other, :, 2 * half :] = marks
    kv_ref[me] = send_ref[col]

    pl.semaphore_wait(barrier, peers - 1)

    def copy_to(peer, peer_row, peer_col):
        return pltpu.make_async_remote_copy(
            src_ref=send_ref.at[peer_col],
            dst_ref=kv_ref.at[me],
            send_sem=send_sem.at[peer],
            recv_sem=recv_sem.at[me],
            device_id={"row": peer_row, "col": peer_col},
            device_id_type=MESH,
        )

    repeat(peers - 1, lambda distance: copy_to(*place(distance)).start())

    def receive(distance):
        peer, peer_row, peer_col = place(distance)
        pltpu.make_async_remote_copy(
            src_ref=send_ref.at[0],
            dst_ref=kv_ref.at[peer],
            send_sem=send_sem.at[peer],
            recv_sem=recv_sem.at[peer],
            device_id={"row": peer_row, "col": peer_col},
            device_id_type=MESH,
        ).wait_recv()

    q_copy.wait()
    repeat(peers - 1, receive)

    marks = kv_ref[:, :, 2 * half :].reshape(keys, DH).astype(jnp.float32)
    lane = lax.broadcasted_iota(jnp.int32, (keys, DH), 1).astype(jnp.float32)
    late = jnp.where(marks > lane, LOW, 0.0).astype(jnp.bfloat16)
    picked = lax.broadcasted_iota(jnp.int32, (DH, query_count), 0) == qstep_ref[...]
    picked = jnp.where(picked, 1.0, 0.0).astype(jnp.bfloat16)
    bias = lax.dot_general(picked, late, (((0,), (1,)), ((), ())), preferred_element_type=jnp.float32)
    first_row = row * query_count
    key_tiles = tile_ref.shape[1]
    block = min(TILE, query_count)
    for part in range(query_count // block):
        tile = (first_row + part * block) // TILE
        for key_tile in range(key_tiles):
            closed = jnp.where(tile_ref[tile, key_tile] == 1, 0.0, LOW)
            span = slice(key_tile * TILE, (key_tile + 1) * TILE)
            bias_ref[part * block : (part + 1) * block, span] = (
                bias[part * block : (part + 1) * block, span] + closed
            )

    scale = math.log2(math.e) / math.sqrt(DH)
    together = max(1, min(groups, 256 // query_count))
    for head in range(heads):
        for start in range(0, groups, together):
            base = (head * groups + start) * DH
            q = jnp.concatenate(
                [q_ref[:, base + g * DH : base + (g + 1) * DH] for g in range(together)], axis=0
            )
            result = attend(q, kv_ref, bias_ref, head, heads, peers, scale).astype(jnp.bfloat16)
            for g in range(together):
                out_ref[:, base + g * DH : base + (g + 1) * DH] = result[
                    g * query_count : (g + 1) * query_count
                ]

    repeat(peers - 1, lambda distance: copy_to(*place(distance)).wait_send())


def solution(mesh):
    row_count, columns = mesh.shape["row"], mesh.shape["col"]
    peers = row_count * columns

    def per_device(queries, key_cache, value_cache, tile_active, query_step, key_step):
        depth = key_cache.shape[0]
        width = 2 * (KVH // columns) * DH + DH
        vmem = pl.BlockSpec(memory_space=pltpu.VMEM)
        return pl.pallas_call(
            functools.partial(kernel, row_count, columns),
            out_shape=jax.ShapeDtypeStruct(queries.shape, jnp.bfloat16),
            in_specs=[
                pl.BlockSpec(memory_space=pl.ANY),
                vmem,
                vmem,
                pl.BlockSpec(memory_space=pltpu.SMEM),
                vmem,
                vmem,
            ],
            out_specs=vmem,
            scratch_shapes=[
                pltpu.VMEM(queries.shape, jnp.bfloat16),
                pltpu.VMEM((columns, depth, width), jnp.bfloat16),
                pltpu.VMEM((peers, depth, width), jnp.bfloat16),
                pltpu.VMEM((queries.shape[0], peers * depth), jnp.float32),
                pltpu.SemaphoreType.DMA,
                pltpu.SemaphoreType.DMA((peers,)),
                pltpu.SemaphoreType.DMA((peers,)),
            ],
            compiler_params=pltpu.CompilerParams(
                collective_id=0, has_side_effects=True, vmem_limit_bytes=48 * 1024 * 1024
            ),
        )(queries, key_cache, value_cache, tile_active, query_step[None, :], key_step[None, :])

    in_specs = (
        P(("grp", "row"), "col"),
        P(("grp", "row", "col"), None),
        P(("grp", "row", "col"), None),
        P("grp", None),
        P(("grp", "row")),
        P(("grp", "row", "col")),
    )
    return jax.shard_map(
        per_device, mesh=mesh, in_specs=in_specs, out_specs=P(("grp", "row"), "col"), check_vma=False
    )
```

time: 107 us -> 19.2 us (0.18)
  the two profiles are of different devices: /device:TPU:0 before, /device:TPU:11 now
where the time goes in v1:
time: 19.2 us; the launch traced here: 18.8 us
  Pallas kernels  14.2 us (74%)
  local copies, waits for them, and re-layouts  4.62 us (24%)
    pallas_call x1, Pallas kernels, per_device(): pl.pallas_call(functools.partial(kernel, row_count, columns), out_shape=j...  14.2 us
    unnamed x14, local copies, waits for them, and re-layouts  4.62 us

profile of v1, /device:TPU:11, one launch (start us, length us, event | category | flops | bytes accessed | tf_op | source)
XLA Modules:
  0.0 18.8 jit_solution(10090233986131985061)
XLA Ops:
  0.0 0.0 copy-start.5
  0.0 0.7 %copy-done.5 = s32[4,2]{0,1:T(2,128)S(1)} copy-done((s32[4,2]{0,1:T(2,128)S(1)}, s32[4,2]{0,1:T(2,128)}, u32[]{:S(2)}) %copy-start.5) | copy-done | bytes 56
  0.7 0.0 copy-start.3
  0.7 0.0 copy-start.4
  0.7 0.1 copy.7.tile_ref
  0.8 0.6 %copy-done.3 = s32[64]{0:T(128)S(1)} copy-done((s32[64]{0:T(128)S(1)}, s32[64]{0:T(128)}, u32[]{:S(2)}) %copy-start.3) | copy-done | bytes 280
  1.3 0.0 copy-done.4
  1.4 0.0 copy-start
  1.4 1.0 %copy-done = bf16[64,4096]{1,0:T(8,128)(2,1)S(1)} copy-done((bf16[64,4096]{1,0:T(8,128)(2,1)S(1)}, bf16[64,4096]{1,0:T(8,128)(2,1)}, u32[]{:S(2)}) %copy-start) | copy-done | bytes 524312
  2.4 0.0 copy-start.1
  2.4 0.7 %copy-done.1 = bf16[16,512]{1,0:T(8,128)(2,1)S(1)} copy-done((bf16[16,512]{1,0:T(8,128)(2,1)S(1)}, bf16[16,512]{1,0:T(8,128)(2,1)}, u32[]{:S(2)}) %copy-start.1) | copy-done | bytes 16408
  3.1 0.0 copy-start.2
  3.1 0.7 %copy-done.2 = bf16[16,512]{1,0:T(8,128)(2,1)S(1)} copy-done((bf16[16,512]{1,0:T(8,128)(2,1)S(1)}, bf16[16,512]{1,0:T(8,128)(2,1)}, u32[]{:S(2)}) %copy-start.2) | copy-done | bytes 16408
  3.8 14.2 %shard_map.64 = bf16[64,4096]{1,0:T(8,128)(2,1)S(1)} custom-call(bf16[64,4096]{1,0:T(8,128)(2,1)S(1)} %copy-done, bf16[16,512]{1,0:T(8,128)(2,1)S(1)} %copy-done.1, bf16[16,512]{1,0:T(8,128)(2,1)S(1)} %copy-done.2, s32[4,2]{1,0:T(4,128)S(1)} %copy.7.tile_ref, s32[1,64]{1,0:T(1,128)S(1)} %bitcast.2, s32[1,16]{1,0:T(1,128)S(1)} %bitcast.3), custom_call_target="tpu_custom_call" | custom-call | tf_op jit(solution)/shard_map/pallas_call | solution.py:179
  18.0 0.8 %copy.9 = bf16[64,4096]{1,0:T(8,128)(2,1)} copy(bf16[64,4096]{1,0:T(8,128)(2,1)S(1)} %shard_map.64) | data formatting | bytes 1048576
Async XLA Ops:
  0.0 0.7 %copy-start.5 = (s32[4,2]{0,1:T(2,128)S(1)}, s32[4,2]{0,1:T(2,128)}, u32[]{:S(2)}) copy-start(s32[4,2]{0,1:T(2,128)} %param.9) | copy-start | bytes 100
  0.7 0.7 %copy-start.3 = (s32[64]{0:T(128)S(1)}, s32[64]{0:T(128)}, u32[]{:S(2)}) copy-start(s32[64]{0:T(128)} %param.10) | copy-start | bytes 772
  0.7 0.7 %copy-start.4 = (s32[16]{0:T(128)S(1)}, s32[16]{0:T(128)}, u32[]{:S(2)}) copy-start(s32[16]{0:T(128)} %param.11) | copy-start | bytes 196
  1.4 1.0 %copy-start = (bf16[64,4096]{1,0:T(8,128)(2,1)S(1)}, bf16[64,4096]{1,0:T(8,128)(2,1)}, u32[]{:S(2)}) copy-start(bf16[64,4096]{1,0:T(8,128)(2,1)} %q_hbm.1) | copy-start | bytes 1572868
  2.4 0.7 %copy-start.1 = (bf16[16,512]{1,0:T(8,128)(2,1)S(1)}, bf16[16,512]{1,0:T(8,128)(2,1)}, u32[]{:S(2)}) copy-start(bf16[16,512]{1,0:T(8,128)(2,1)} %k_ref.1) | copy-start | bytes 49156
  3.1 0.7 %copy-start.2 = (bf16[16,512]{1,0:T(8,128)(2,1)S(1)}, bf16[16,512]{1,0:T(8,128)(2,1)}, u32[]{:S(2)}) copy-start(bf16[16,512]{1,0:T(8,128)(2,1)} %v_ref.1) | copy-start | bytes 49156

commit v2 on v1

--- a/solution.py
+++ b/solution.py
@@ -66,22 +66,30 @@
 
 
 def kernel(
-    row_count, columns, q_hbm, k_ref, v_ref, tile_ref, qstep_ref, kstep_ref, out_ref,
-    q_ref, send_ref, kv_ref, bias_ref, q_sem, send_sem, recv_sem,
+    row_count, columns, q_hbm, k_hbm, v_hbm, tile_hbm, qstep_hbm, kstep_hbm, out_ref,
+    q_ref, send_ref, kv_ref, bias_ref, tile_ref, qstep_ref, kstep_ref, load_sem, send_sem, recv_sem,
 ):
     peers = row_count * columns
     heads = KVH // columns
     half = heads * DH
     groups = H // KVH
-    depth = k_ref.shape[0]
+    depth = k_hbm.shape[0]
     keys = peers * depth
     query_count = q_ref.shape[0]
     row = lax.axis_index("row")
     col = lax.axis_index("col")
     me = row * columns + col
 
-    q_copy = pltpu.make_async_copy(q_hbm, q_ref, q_sem)
-    q_copy.start()
+    def load(source, target, index):
+        copy = pltpu.make_async_copy(source, target, load_sem.at[index])
+        copy.start()
+        return copy
+
+    own_loads = [load(kstep_hbm, kstep_ref, 0)]
+    for other in range(columns):
+        span = slice(other * half, (other + 1) * half)
+        own_loads.append(load(k_hbm.at[:, span], send_ref.at[other, :, pl.ds(0, half)], 4 + 2 * other))
+        own_loads.append(load(v_hbm.at[:, span], send_ref.at[other, :, pl.ds(half, half)], 5 + 2 * other))
 
     def place(distance):
         peer = lax.rem(me + distance + 1, peers)
@@ -95,16 +103,16 @@
 
     repeat(peers - 1, greet)
 
+    other_loads = [load(q_hbm, q_ref, 1), load(qstep_hbm, qstep_ref, 2), load(tile_hbm, tile_ref, 3)]
+    own_loads[0].wait()
     steps = kstep_ref[...].astype(jnp.float32)
     eye = lax.broadcasted_iota(jnp.int32, (depth, depth), 0) == lax.broadcasted_iota(jnp.int32, (depth, depth), 1)
     column = jnp.sum(jnp.where(eye, jnp.broadcast_to(steps, (depth, depth)), 0.0), axis=1, keepdims=True)
     marks = jnp.broadcast_to(column, (depth, DH)).astype(jnp.bfloat16)
     for other in range(columns):
-        send_ref[other, :, :half] = k_ref[:, other * half : (other + 1) * half]
-        send_ref[other, :, half : 2 * half] = v_ref[:, other * half : (other + 1) * half]
         send_ref[other, :, 2 * half :] = marks
-    kv_ref[me] = send_ref[col]
-
+    for copy in own_loads[1:]:
+        copy.wait()
     pl.semaphore_wait(barrier, peers - 1)
 
     def copy_to(peer, peer_row, peer_col):
@@ -130,7 +138,9 @@
             device_id_type=MESH,
         ).wait_recv()
 
-    q_copy.wait()
+    kv_ref[me] = send_ref[col]
+    for copy in other_loads:
+        copy.wait()
     repeat(peers - 1, receive)
 
     marks = kv_ref[:, :, 2 * half :].reshape(keys, DH).astype(jnp.float32)
@@ -140,12 +150,12 @@
     picked = jnp.where(picked, 1.0, 0.0).astype(jnp.bfloat16)
     bias = lax.dot_general(picked, late, (((0,), (1,)), ((), ())), preferred_element_type=jnp.float32)
     first_row = row * query_count
-    key_tiles = tile_ref.shape[1]
+    key_tiles = tile_ref.shape[0]
     block = min(TILE, query_count)
     for part in range(query_count // block):
         tile = (first_row + part * block) // TILE
         for key_tile in range(key_tiles):
-            closed = jnp.where(tile_ref[tile, key_tile] == 1, 0.0, LOW)
+            closed = jnp.where(tile_ref[key_tile, tile] == 1, 0.0, LOW)
             span = slice(key_tile * TILE, (key_tile + 1) * TILE)
             bias_ref[part * block : (part + 1) * block, span] = (
                 bias[part * block : (part + 1) * block, span] + closed
@@ -179,28 +189,24 @@
         return pl.pallas_call(
             functools.partial(kernel, row_count, columns),
             out_shape=jax.ShapeDtypeStruct(queries.shape, jnp.bfloat16),
-            in_specs=[
-                pl.BlockSpec(memory_space=pl.ANY),
-                vmem,
-                vmem,
-                pl.BlockSpec(memory_space=pltpu.SMEM),
-                vmem,
-                vmem,
-            ],
+            in_specs=[pl.BlockSpec(memory_space=pltpu.HBM)] * 6,
             out_specs=vmem,
             scratch_shapes=[
                 pltpu.VMEM(queries.shape, jnp.bfloat16),
                 pltpu.VMEM((columns, depth, width), jnp.bfloat16),
                 pltpu.VMEM((peers, depth, width), jnp.bfloat16),
                 pltpu.VMEM((queries.shape[0], peers * depth), jnp.float32),
-                pltpu.SemaphoreType.DMA,
+                pltpu.SMEM(tile_active.shape[::-1], jnp.int32),
+                pltpu.VMEM((1, query_step.shape[0]), jnp.int32),
+                pltpu.VMEM((1, depth), jnp.int32),
+                pltpu.SemaphoreType.DMA((4 + 2 * columns,)),
                 pltpu.SemaphoreType.DMA((peers,)),
                 pltpu.SemaphoreType.DMA((peers,)),
             ],
             compiler_params=pltpu.CompilerParams(
-                collective_id=0, has_side_effects=True, vmem_limit_bytes=48 * 1024 * 1024
+                collective_id=0, has_side_effects=True, vmem_limit_bytes=64 * 1024 * 1024
             ),
-        )(queries, key_cache, value_cache, tile_active, query_step[None, :], key_step[None, :])
+        )(queries, key_cache, value_cache, tile_active.T, query_step[None, :], key_step[None, :])
 
     in_specs = (
         P(("grp", "row"), "col"),

time: 19.2 us -> 16.4 us (0.85); the launches traced: 18.8 us -> 16.2 us
  local copies, waits for them, and re-layouts: 4.62 us -> 1.87 us
    unnamed x14 -> x1, local copies, waits for them, and re-layouts: 4.62 us -> 1.87 us
where the time goes in v2:
time: 16.4 us; the launch traced here: 16.2 us
  Pallas kernels  14.3 us (87%)
  local copies, waits for them, and re-layouts  1.87 us (11%)
    pallas_call x1, Pallas kernels, per_device(): pl.pallas_call(functools.partial(kernel, row_count, columns), out_shape=j...  14.3 us
    unnamed x1, local copies, waits for them, and re-layouts  1.87 us

profile of v2, /device:TPU:11, one launch (start us, length us, event | category | flops | bytes accessed | tf_op | source)
XLA Modules:
  0.0 16.2 jit_solution(5892578478946803727)
XLA Ops:
  0.0 14.3 %shard_map.64 = bf16[64,4096]{1,0:T(8,128)(2,1)} custom-call(bf16[64,4096]{1,0:T(8,128)(2,1)} %q_hbm.1, bf16[16,512]{1,0:T(8,128)(2,1)} %k_hbm.1, bf16[16,512]{1,0:T(8,128)(2,1)} %v_hbm.1, s32[2,4]{1,0:T(2,128)} %bitcast.3, s32[1,64]{1,0:T(1,128)} %bitcast.4, s32[1,16]{1,0:T(1,128)} %bitcast.5), custom_call_target="tpu_custom_call" | custom-call | tf_op jit(solution)/shard_map/pallas_call | solution.py:189
  14.3 1.9 %copy.8 = bf16[64,4096]{1,0:T(8,128)(2,1)} copy(bf16[64,4096]{1,0:T(8,128)(2,1)} %shard_map.64) | data formatting | bytes 1048576
